TPU v7x, 256 devices: a whole 4x4x8 slice. The times are simulated.
256 devices in a mesh: dp: 32 (over z, x), head: 8 (over y, core).
Axes of the slice: x: 4, y: 4, z: 8, core: 2. Of those that a mesh axis runs over, the one named last changes fastest.
Arguments:
- queries: bfloat16 [5120, 128, 192], P(('dp', 'head')), may hold values from -6 to 6
- latents: bfloat16 [5120, 576], P('dp'), may hold values from -6 to 6
- cache_pool: bfloat16 [1024, 64, 576], P('dp'), may hold values from -6 to 6
- key_up: bfloat16 [128, 128, 512], P('head'), may hold values from -0.5 to 0.5
- value_up: bfloat16 [128, 512, 128], P('head'), may hold values from -0.25 to 0.25
- prefix_rank: int32 [1024, 1], P('dp'), may hold values from 0 to 31; in each aligned block of 32 rows (0 to 31, 32 to 63, ...) at most 2 rows name the same one
- prefix_block: int32 [1024], P('dp'), may hold values from 0 to 31
- decode_start: int32 [1024], P('dp'), may hold values from 0 to 1536
- decode_length: int32 [1024], P('dp'), may hold values from 1 to 512, as said below
Outputs:
- head_values: bfloat16 [5120, 128, 128], P(('dp', 'head'))
Inputs may be any that keep to these rules, and one draw needn't show every extreme that they name: `prefix_rank`: among the 32 rows of one dp rank no rank is named more than 2 times. `decode_length`: every dp rank has a decode row of length 512.
All inputs are finite; a program needn't handle non-finite values.
Results may differ from a plain program's by a relative error of at most 0.0066.
Values may be sent and summed in bfloat16 or wider, within the bound.
A program may use at most 64 MiB of HBM per device.

v0:
```python
import math

import jax
import jax.numpy as jnp
from jax import lax
from jax.sharding import PartitionSpec as P


def ranks_within(sources):
    count_rows = sources.shape[-1]
    indices = jnp.arange(count_rows)
    same_source = sources[..., :, None] == sources[..., None, :]
    earlier = indices[None, :] < indices[:, None]
    return jnp.sum(jnp.where(same_source & earlier, 1, 0), axis=-1).astype(jnp.int32)


def two_part_mix(scores_first, keys_first, scores_second, keys_second, latent_dim):
    row_peak = jnp.maximum(
        jnp.max(scores_first, axis=1, keepdims=True), jnp.max(scores_second, axis=1, keepdims=True)
    )
    raised_first = jnp.exp(scores_first - row_peak)
    raised_second = jnp.exp(scores_second - row_peak)
    denominator = jnp.sum(raised_first, axis=1, keepdims=True) + jnp.sum(
        raised_second, axis=1, keepdims=True
    )
    mixed_first = jnp.dot(
        raised_first.astype(jnp.bfloat16), keys_first, preferred_element_type=jnp.float32
    )
    mixed_second = jnp.dot(
        raised_second.astype(jnp.bfloat16), keys_second, preferred_element_type=jnp.float32
    )
    return (mixed_first + mixed_second)[:, :latent_dim] / denominator


def body(
    queries,
    latents,
    cache_pool,
    key_up,
    value_up,
    prefix_rank,
    prefix_block,
    decode_start,
    decode_length,
):
    grouped = lax.all_to_all(queries, "head", split_axis=1, concat_axis=0, tiled=True)
    nope_dim = key_up.shape[1]
    latent_dim = key_up.shape[2]
    width_all = cache_pool.shape[2]
    block_rows = cache_pool.shape[1]
    scale_value = float(grouped.shape[2]) ** (-0.5)
    absorbed = jnp.einsum(
        "rhn,hnc->rhc", grouped[:, :, :nope_dim], key_up, preferred_element_type=jnp.float32
    ).astype(jnp.bfloat16)
    query_cat = jnp.concatenate([absorbed, grouped[:, :, nope_dim:]], axis=2)
    rank_count = lax.axis_size("dp")
    prefix_count = prefix_block.shape[0]
    capacity = max(2, 2 * prefix_count // rank_count)
    sources = prefix_rank[:, 0]
    within = ranks_within(sources)
    slot_range = jnp.arange(capacity)
    matches = (sources[:, None, None] == jnp.arange(rank_count)[None, :, None]) & (
        within[:, None, None] == slot_range[None, None, :]
    )
    wanted = jnp.sum(jnp.where(matches, prefix_block[:, None, None] + 1, 0), axis=0) - 1
    asked_ids = lax.all_to_all(wanted, "dp", split_axis=0, concat_axis=0, tiled=True)
    safe_ids = jnp.maximum(asked_ids, 0)
    outgoing = cache_pool[safe_ids]
    arrived = lax.all_to_all(outgoing, "dp", split_axis=0, concat_axis=0, tiled=True)
    prefix_keys = arrived[sources, within].reshape(prefix_count * block_rows, width_all)
    decode_rows = decode_start.shape[0]
    total_rows = grouped.shape[0]
    prefill_rows = total_rows - decode_rows
    heads_here = grouped.shape[1]
    flat_rows = prefill_rows * heads_here
    block_size = math.gcd(flat_rows, 512)
    block_count = flat_rows // block_size
    prefill_query = query_cat[:prefill_rows].reshape(block_count, block_size, width_all)
    row_position = (jnp.arange(flat_rows) // heads_here).reshape(block_count, block_size)
    local_keys = latents[:prefill_rows]
    local_index = jnp.arange(prefill_rows)

    def prefill_block(block_item):
        block_query, block_position = block_item
        scores_prefix = (
            jnp.einsum("qd,kd->qk", block_query, prefix_keys, preferred_element_type=jnp.float32)
            * scale_value
        )
        scores_local = (
            jnp.einsum("qd,kd->qk", block_query, local_keys, preferred_element_type=jnp.float32)
            * scale_value
        )
        scores_local = jnp.where(
            local_index[None, :] <= block_position[:, None], scores_local, -jnp.inf
        )
        return two_part_mix(scores_prefix, prefix_keys, scores_local, local_keys, latent_dim)

    prefill_mixed = lax.map(prefill_block, (prefill_query, row_position)).reshape(
        prefill_rows, heads_here, latent_dim
    )
    flat_cache = cache_pool.reshape(-1, width_all)
    cache_index = jnp.arange(flat_cache.shape[0])
    own_keys = latents[prefill_rows:]
    decode_flat = decode_rows * heads_here
    decode_size = math.gcd(decode_flat, 512)
    decode_count = decode_flat // decode_size
    decode_query = query_cat[prefill_rows:].reshape(decode_count, decode_size, width_all)
    row_start = jnp.broadcast_to(decode_start[:, None], (decode_rows, heads_here)).reshape(
        decode_count, decode_size
    )
    row_length = jnp.broadcast_to(decode_length[:, None], (decode_rows, heads_here)).reshape(
        decode_count, decode_size
    )
    row_owner = (jnp.arange(decode_flat) // heads_here).reshape(decode_count, decode_size)

    def decode_block(decode_item):
        block_query, first_row, length, owner = decode_item
        scores_cache = (
            jnp.einsum("qd,kd->qk", block_query, flat_cache, preferred_element_type=jnp.float32)
            * scale_value
        )
        offset = cache_index[None, :] - first_row[:, None]
        visible = (offset >= 0) & (offset < length[:, None])
        scores_cache = jnp.where(visible, scores_cache, -jnp.inf)
        owner_match = (owner[:, None] == jnp.arange(decode_rows)[None, :]).astype(jnp.bfloat16)
        row_keys = jnp.dot(owner_match, own_keys, preferred_element_type=jnp.float32).astype(
            jnp.bfloat16
        )
        score_own = (
            jnp.sum(
                block_query.astype(jnp.float32) * row_keys.astype(jnp.float32),
                axis=1,
                keepdims=True,
            )
            * scale_value
        )
        row_peak = jnp.maximum(jnp.max(scores_cache, axis=1, keepdims=True), score_own)
        raised_cache = jnp.exp(scores_cache - row_peak)
        raised_own = jnp.exp(score_own - row_peak)
        denominator = jnp.sum(raised_cache, axis=1, keepdims=True) + raised_own
        mixed = jnp.dot(
            raised_cache.astype(jnp.bfloat16), flat_cache, preferred_element_type=jnp.float32
        )[:, :latent_dim]
        mixed = mixed + raised_own.astype(jnp.bfloat16).astype(jnp.float32) * row_keys[
            :, :latent_dim
        ].astype(jnp.float32)
        return mixed / denominator

    decode_mixed = lax.map(decode_block, (decode_query, row_start, row_length, row_owner)).reshape(
        decode_rows, heads_here, latent_dim
    )
    mixed_latent = jnp.concatenate([prefill_mixed, decode_mixed], axis=0).astype(jnp.bfloat16)
    head_values = jnp.einsum(
        "rhc,hcv->rhv", mixed_latent, value_up, preferred_element_type=jnp.float32
    ).astype(jnp.bfloat16)
    return lax.all_to_all(head_values, "head", split_axis=0, concat_axis=1, tiled=True)


def solution(mesh):
    return jax.shard_map(
        body,
        mesh=mesh,
        in_specs=(
            P(("dp", "head"), None, None),
            P("dp", None),
            P("dp", None, None),
            P("head", None, None),
            P("head", None, None),
            P("dp", None),
            P("dp"),
            P("dp"),
            P("dp"),
        ),
        out_specs=P(("dp", "head"), None, None),
        check_vma=False,
    )
```

profile of v0, /device:TPU:1, one launch (start us, length us, event | category | flops | bytes accessed | tf_op | source)
XLA Modules:
  0.0 241.4 jit_solution(9280306434542633824)
XLA Ops:
  3.2 11.9 %all-to-all-start.1 = ((s32[32,1,2]{2,1,0:T(1,128)}), s32[32,1,2]{2,1,0:T(1,128)S(1)}, u32[]{:S(2)}, u32[]{:S(2)}) async-start(s32[32,1,2]{2,1,0:T(1,128)} %copy.63), calls=%async_computation.1 | async-start | bytes 32768 | tf_op jit(solution)/shard_map/all_to_all | solution.py:66
  15.1 2.8 %copy.57 = bf16[20,128,192]{2,0,1:T(8,128)(2,1)} copy(bf16[20,128,192]{1,2,0:T(8,128)(2,1)} %param.11) | data formatting | bytes 1966080 | tf_op args[0]
  17.9 5.7 %all-to-all-done.1 = s32[32,1,2]{2,1,0:T(1,128)S(1)} async-done(((s32[32,1,2]{2,1,0:T(1,128)}), s32[32,1,2]{2,1,0:T(1,128)S(1)}, u32[]{:S(2)}, u32[]{:S(2)}) %all-to-all-start.1) | async-done | bytes 288 | tf_op jit(solution)/shard_map/all_to_all | solution.py:66
  23.6 6.6 %all-to-all-start = ((bf16[20,128,192]{2,0,1:T(8,128)(2,1)}), bf16[20,128,192]{2,0,1:T(8,128)(2,1)}, u32[]{:S(2)}, u32[]{:S(2)}) async-start(bf16[20,128,192]{2,0,1:T(8,128)(2,1)} %copy.57), calls=%async_computation | async-start | bytes 3145728 | tf_op jit(solution)/shard_map/all_to_all | solution.py:46
  30.3 5.3 %gather_fusion = bf16[64,64,576]{2,1,0:T(8,128)(2,1)} fusion(bf16[32,64,576]{2,1,0:T(8,128)(2,1)} %param.13, s32[1024]{0:T(1024)S(1)} %pad_clamp_fusion), kind=kCustom, calls=%fused_computation | custom fusion | bytes 9437440 | tf_op jit(solution)/shard_map/gather | solution.py:68
  35.6 15.4 %all-to-all-done = bf16[20,128,192]{2,0,1:T(8,128)(2,1)} async-done(((bf16[20,128,192]{2,0,1:T(8,128)(2,1)}), bf16[20,128,192]{2,0,1:T(8,128)(2,1)}, u32[]{:S(2)}, u32[]{:S(2)}) %all-to-all-start) | async-done | bytes 983072 | tf_op jit(solution)/shard_map/all_to_all | solution.py:46
  51.0 5.2 %all-to-all-start.2 = ((bf16[32,2,64,576]{3,2,1,0:T(8,128)(2,1)}), bf16[32,2,64,576]{3,2,1,0:T(8,128)(2,1)}, u32[]{:S(2)}, u32[]{:S(2)}) async-start(bf16[32,2,64,576]{3,2,1,0:T(8,128)(2,1)} %bitcast.66), calls=%async_computation.2 | async-start | bytes 10485760 | tf_op jit(solution)/shard_map/all_to_all | solution.py:69
  64.7 4.2 %fusion.79 = (f32[512]{0:T(512)S(1)}, f32[512,2048]{1,0:T(8,128)S(1)}) fusion(bf16[512,576]{1,0:T(8,128)(2,1)} %bitcast.74, bf16[2048,576]{1,0:T(8,128)(2,1)} %bitcast.67, s32[512]{0:T(512)} %lt.51, s32[512]{0:T(512)} %sub.84), kind=kOutput, calls=%fused_computation.102 | convolution fusion | flops 1215299072 | bytes 7149568 | tf_op jit(solution)/shard_map/while/body/eval_jaxpr/qd,kd->qk/dot_general | solution.py:119
  70.7 2.2 fusion.55
  75.2 1.9 fusion.30
  77.1 3.0 %copy.62 = bf16[128,16,576]{2,1,0:T(8,128)(2,1)} copy(bf16[128,16,576]{2,0,1:T(8,128)(2,1)S(1)} %fusion.30) | data formatting | bytes 4718592 | tf_op jit(solution)/shard_map/slice | solution.py:78
  80.1 90.9 %all-to-all-done.2 = bf16[32,2,64,576]{3,2,1,0:T(8,128)(2,1)} async-done(((bf16[32,2,64,576]{3,2,1,0:T(8,128)(2,1)}), bf16[32,2,64,576]{3,2,1,0:T(8,128)(2,1)}, u32[]{:S(2)}, u32[]{:S(2)}) %all-to-all-start.2) | async-done | bytes 4718624 | tf_op jit(solution)/shard_map/all_to_all | solution.py:69
  171.0 4.9 %gather_fusion.1 = bf16[32,64,576]{2,1,0:T(8,128)(2,1)} fusion(bf16[32,2,64,576]{3,2,1,0:T(8,128)(2,1)} %all-to-all-done.2, s32[32]{0:T(128)S(1)} %fusion.75), kind=kCustom, calls=%fused_computation.1 | custom fusion | bytes 4718848 | tf_op jit(solution)/shard_map/gather | solution.py:70
  175.9 44.3 %while.3 = (s32[]{:T(128)}, bf16[4,512,512]{2,1,0:T(8,128)(2,1)}, bf16[4,512,576]{2,1,0:T(8,128)(2,1)}, bf16[2048,576]{1,0:T(8,128)(2,1)}, s32[4,512]{1,0:T(4,128)}, /*index=5*/bf16[128,576]{1,0:T(8,128)(2,1)S(1)}, s32[]{:T(128)}) while((s32[]{:T(128)}, bf16[4,512,512]{2,1,0:T(8,128)(2,1)}, bf16[4,512,576]{2,1,0:T(8,128)(2,1)}, ...), condition=%wide.region_7.8_spmd.clone, body=%wide.region_2.7_spmd.clone.sunk | while | flops 2576350208 | bytes 34936428 | solution.py:98
  178.0 3.9 %multiply_reduce_fusion.3 = (f32[512]{0:T(512)S(1)}, f32[512,2048]{1,0:T(8,128)S(1)}) fusion(bf16[2048,576]{1,0:T(8,128)(2,1)} %get-tuple-element.168, bf16[4,512,576]{2,1,0:T(8,128)(2,1)} %get-tuple-element.167, s32[]{:T(128)} %get-tuple-element.158), kind=kOutput, calls=%fused_computation.4.clone.1 | convolution fusion | flops 1210056192 | bytes 7473664 | tf_op jit(solution)/shard_map/while/body/eval_jaxpr/qd,kd->qk/dot_general | solution.py:86
  183.7 1.9 fusion.108
  189.2 3.9 %multiply_reduce_fusion.3 = (f32[512]{0:T(512)S(1)}, f32[512,2048]{1,0:T(8,128)S(1)}) fusion(bf16[2048,576]{1,0:T(8,128)(2,1)} %get-tuple-element.168, bf16[4,512,576]{2,1,0:T(8,128)(2,1)} %get-tuple-element.167, s32[]{:T(128)} %get-tuple-element.158), kind=kOutput, calls=%fused_computation.4.clone.1 | convolution fusion | flops 1210056192 | bytes 7473664 | tf_op jit(solution)/shard_map/while/body/eval_jaxpr/qd,kd->qk/dot_general | solution.py:86
  194.8 1.9 fusion.108
  200.2 3.9 %multiply_reduce_fusion.3 = (f32[512]{0:T(512)S(1)}, f32[512,2048]{1,0:T(8,128)S(1)}) fusion(bf16[2048,576]{1,0:T(8,128)(2,1)} %get-tuple-element.168, bf16[4,512,576]{2,1,0:T(8,128)(2,1)} %get-tuple-element.167, s32[]{:T(128)} %get-tuple-element.158), kind=kOutput, calls=%fused_computation.4.clone.1 | convolution fusion | flops 1210056192 | bytes 7473664 | tf_op jit(solution)/shard_map/while/body/eval_jaxpr/qd,kd->qk/dot_general | solution.py:86
  205.8 1.9 fusion.108
  211.3 3.9 %multiply_reduce_fusion.3 = (f32[512]{0:T(512)S(1)}, f32[512,2048]{1,0:T(8,128)S(1)}) fusion(bf16[2048,576]{1,0:T(8,128)(2,1)} %get-tuple-element.168, bf16[4,512,576]{2,1,0:T(8,128)(2,1)} %get-tuple-element.167, s32[]{:T(128)} %get-tuple-element.158), kind=kOutput, calls=%fused_computation.4.clone.1 | convolution fusion | flops 1210056192 | bytes 7473664 | tf_op jit(solution)/shard_map/while/body/eval_jaxpr/qd,kd->qk/dot_general | solution.py:86
  216.9 1.9 fusion.108
  220.2 2.9 %copy.68 = bf16[128,16,512]{2,0,1:T(8,128)(2,1)S(1)} copy(bf16[128,16,512]{2,1,0:T(8,128)(2,1)} %bitcast.12) | data formatting | bytes 4194304 | tf_op jit(solution)/shard_map/reshape | solution.py:98
  224.2 16.1 %all_to_all.47 = bf16[160,16,128]{2,1,0:T(8,128)(2,1)S(1)} all-to-all(bf16[160,16,128]{2,1,0:T(8,128)(2,1)S(1)} %copy.70), channel_id=1, replica_groups=mesh['dp'=32,'head'=8] {'head'}, dimensions={0} | all-to-all | bytes 1310720 | tf_op jit(solution)/shard_map/all_to_all | solution.py:156
  (95 shorter events, 38.9 us)
Async XLA Ops:
  0.0 60.4 %copy-start = (bf16[16,128,512]{2,1,0:T(8,128)(2,1)S(1)}, bf16[16,128,512]{2,1,0:T(8,128)(2,1)}, u32[]{:S(2)}) copy-start(bf16[16,128,512]{2,1,0:T(8,128)(2,1)} %param.14) | copy-start | bytes 6291460
  3.2 20.4 %all-to-all-start.1 = ((s32[32,1,2]{2,1,0:T(1,128)}), s32[32,1,2]{2,1,0:T(1,128)S(1)}, u32[]{:S(2)}, u32[]{:S(2)}) async-start(s32[32,1,2]{2,1,0:T(1,128)} %copy.63), calls=%async_computation.1 | async-start | bytes 32768 | tf_op jit(solution)/shard_map/all_to_all | solution.py:66
  23.6 27.4 %all-to-all-start = ((bf16[20,128,192]{2,0,1:T(8,128)(2,1)}), bf16[20,128,192]{2,0,1:T(8,128)(2,1)}, u32[]{:S(2)}, u32[]{:S(2)}) async-start(bf16[20,128,192]{2,0,1:T(8,128)(2,1)} %copy.57), calls=%async_computation | async-start | bytes 3145728 | tf_op jit(solution)/shard_map/all_to_all | solution.py:46
  51.0 5.2 %copy-start.6 = (s32[32]{0:T(128)S(1)}, s32[32]{0:T(128)}, u32[]{:S(2)}) copy-start(s32[32]{0:T(128)} %param.19) | copy-start | bytes 388
  51.0 5.9 %copy-start.7 = (s32[32]{0:T(128)S(1)}, s32[32]{0:T(128)}, u32[]{:S(2)}) copy-start(s32[32]{0:T(128)} %param.18) | copy-start | bytes 388
  51.0 7.3 %copy-start.8 = (s32[32,1]{0,1:T(1,128)S(1)}, s32[32,1]{0,1:T(1,128)}, u32[]{:S(2)}) copy-start(s32[32,1]{0,1:T(1,128)} %param.16) | copy-start | bytes 388
  51.0 120.0 %all-to-all-start.2 = ((bf16[32,2,64,576]{3,2,1,0:T(8,128)(2,1)}), bf16[32,2,64,576]{3,2,1,0:T(8,128)(2,1)}, u32[]{:S(2)}, u32[]{:S(2)}) async-start(bf16[32,2,64,576]{3,2,1,0:T(8,128)(2,1)} %bitcast.66), calls=%async_computation.2 | async-start | bytes 10485760 | tf_op jit(solution)/shard_map/all_to_all | solution.py:69
  61.2 1.7 copy-start.1
  61.2 3.0 %copy-start.3 = (bf16[160,576]{1,0:T(8,128)(2,1)S(1)}, bf16[160,576]{1,0:T(8,128)(2,1)}, u32[]{:S(2)}) copy-start(bf16[160,576]{1,0:T(8,128)(2,1)} %param.12) | copy-start | bytes 552964
  68.9 1.7 copy-start.2
  80.1 95.8 %slice-start = ((bf16[160,576]{1,0:T(8,128)(2,1)}), bf16[128,576]{1,0:T(8,128)(2,1)S(1)}, s32[]{:S(2)}) async-start(bf16[160,576]{1,0:T(8,128)(2,1)} %param.12), calls=%async_computation.4 | async-start | bytes 327680 | tf_op jit(solution)/shard_map/slice | solution.py:80
  181.9 1.7 copy-start.4
  193.0 1.7 copy-start.4
  204.1 1.7 copy-start.4
  215.1 1.7 copy-start.4
  220.2 2.9 %copy-start.5 = (bf16[32,16,512]{2,0,1:T(8,128)(2,1)S(1)}, bf16[32,16,512]{2,0,1:T(8,128)(2,1)}, u32[]{:S(2)}) copy-start(bf16[32,16,512]{2,0,1:T(8,128)(2,1)} %copy.69) | copy-start | bytes 1572868
  220.2 2.9 %copy-start.9 = (bf16[16,512,128]{2,1,0:T(8,128)(2,1)S(1)}, bf16[16,512,128]{2,1,0:T(8,128)(2,1)}, u32[]{:S(2)}) copy-start(bf16[16,512,128]{2,1,0:T(8,128)(2,1)} %param.15) | copy-start | bytes 6291460
where the time goes:
time: 245 us; the launch traced here: 241 us
  waiting for transfers between devices  112 us (46%)
  matrix products  39 us (16%)
  local copies, waits for them, and re-layouts  36.9 us (15%)
  starting transfers between devices  23.6 us (10%)
  blocking collectives  16.1 us (7%)
  other arithmetic  13.4 us (5%)
    all_to_all x1, waiting for transfers between devices, body(): lax.all_to_all(outgoing, 'dp', split_axis=0, concat_axis=0, tiled=True)  90.9 us
    all_to_all x1, blocking collectives, body(): lax.all_to_all(head_values, 'head', split_axis=0, concat_axis=1, tiled=True)  16.1 us
    dot_general x4, matrix products, prefill_block(): jnp.einsum('qd,kd->qk', block_query, prefix_keys, preferred_element_type=...  15.5 us
    all_to_all x1, waiting for transfers between devices, body(): lax.all_to_all(queries, 'head', split_axis=1, concat_axis=0, tiled=True)  15.4 us
    all_to_all x1, starting transfers between devices, body(): lax.all_to_all(wanted, 'dp', split_axis=0, concat_axis=0, tiled=True)  11.9 us
    dot_general x4, matrix products, two_part_mix(): jnp.dot(raised_first.astype(jnp.bfloat16), keys_first, preferred_element_...  7.76 us
    all_to_all x1, starting transfers between devices, body(): lax.all_to_all(queries, 'head', split_axis=1, concat_axis=0, tiled=True)  6.57 us
    dot_general x4, matrix products, prefill_block(): jnp.einsum('qd,kd->qk', block_query, local_keys, preferred_element_type=j...  5.78 us
  transfers between devices with their start and end apart: 3, of which 3 were waited for; matrix products, arithmetic and copies ran while one was open for 13% of the time, Pallas kernels for 0%

commit v1 on v0

v1 whole, which is shorter than its diff:
```python
import functools
import math

import jax
import jax.numpy as jnp
from jax import lax
from jax.experimental import pallas as pl
from jax.experimental.pallas import tpu as pltpu
from jax.sharding import PartitionSpec as P

MESH = pl.DeviceIdType.MESH
CAP = 2
F32 = jnp.float32
BF16 = jnp.bfloat16
HIDDEN = -1e30


def iota(shape, dim):
    return lax.broadcasted_iota(jnp.int32, shape, dim)


def wait_bytes(ref, sem):
    pltpu.make_async_copy(ref, ref, sem).wait()


def gather_kernel(
    q_ref, cache_ref, rank_ref, block_ref, qg_ref, keys_ref,
    table, ids, rows_here, outgoing, arrived, chunk,
    local_sem, id_send, id_recv, q_send, q_recv, row_send, row_recv, ag_send, ag_recv,
):
    nd, nh = lax.axis_size("dp"), lax.axis_size("head")
    me, hd = lax.axis_index("dp"), lax.axis_index("head")
    chip, core = hd // 2, hd % 2
    blocks, block_rows, width = cache_ref.shape
    part = block_rows // nh
    pair = CAP * part
    q_rows = q_ref.shape[0]
    heads = qg_ref.shape[1]
    reqs = rank_ref.shape[0]
    sibling = chip * 2 + 1 - core

    rows_copy = pltpu.make_async_copy(
        cache_ref.at[:, pl.ds(pl.multiple_of(chip * pair, pair), pair), :], rows_here, local_sem.at[0]
    )
    rows_copy.start()
    barrier = pltpu.get_barrier_semaphore()

    def greet_dp(step, carry):
        peer = lax.rem(me + step, nd)
        pl.semaphore_signal(barrier, inc=1, device_id=(peer, hd), device_id_type=MESH)
        return carry

    def greet_head(step, carry):
        peer = lax.rem(hd + step, nh)
        pl.semaphore_signal(barrier, inc=1, device_id=(me, peer), device_id_type=MESH)
        return carry

    lax.fori_loop(1, nd, greet_dp, 0)
    lax.fori_loop(1, nh, greet_head, 0)

    rank_col = rank_ref[...].astype(F32)
    row_i, col_i = iota((reqs, reqs), 0), iota((reqs, reqs), 1)
    rank_row = jnp.sum(jnp.where(row_i == col_i, rank_col, 0.0), axis=0, keepdims=True)
    same = rank_col == rank_row
    within_row = jnp.sum(jnp.where(same & (row_i < col_i), 1.0, 0.0), axis=0, keepdims=True)
    within_col = jnp.sum(jnp.where(same & (col_i < row_i), 1.0, 0.0), axis=1, keepdims=True)
    block_row = block_ref[...].astype(F32) + 1.0
    hit = rank_row == iota((nd, reqs), 0).astype(F32)
    want0 = jnp.sum(jnp.where(hit & (within_row == 0.0), block_row, 0.0), axis=1, keepdims=True) - 1.0
    want1 = jnp.sum(jnp.where(hit & (within_row == 1.0), block_row, 0.0), axis=1, keepdims=True) - 1.0
    lane = iota((nd, 128), 1)
    table[:, 0, :] = jnp.where(lane == 0, want0, jnp.where(lane == 1, want1, 0.0))

    pl.semaphore_wait(barrier, nd - 1 + nh - 1)

    def send_ids(step, carry):
        peer = lax.rem(me + step, nd)
        pltpu.make_async_remote_copy(
            src_ref=table.at[peer], dst_ref=ids.at[me], send_sem=id_send, recv_sem=id_recv,
            device_id=(peer, hd), device_id_type=MESH,
        ).start()
        return carry

    lax.fori_loop(1, nd, send_ids, 0)
    own_ids = pltpu.make_async_copy(table.at[me], ids.at[me], local_sem.at[1])
    own_ids.start()

    def send_q(step, carry):
        peer = lax.rem(hd + step, nh)
        pltpu.make_async_remote_copy(
            src_ref=q_ref.at[:, pl.ds(pl.multiple_of(peer * heads, heads), heads), :],
            dst_ref=qg_ref.at[pl.ds(hd * q_rows, q_rows)], send_sem=q_send, recv_sem=q_recv,
            device_id=(me, peer), device_id_type=MESH,
        ).start()
        return carry

    lax.fori_loop(1, nh, send_q, 0)
    own_q = pltpu.make_async_copy(
        q_ref.at[:, pl.ds(pl.multiple_of(hd * heads, heads), heads), :],
        qg_ref.at[pl.ds(hd * q_rows, q_rows)], local_sem.at[2],
    )
    own_q.start()

    own_ids.wait()
    wait_bytes(ids.at[pl.ds(0, nd - 1)], id_recv)
    rows_copy.wait()
    total = nd * pair
    expand = (iota((total, nd), 0) // pair == iota((total, nd), 1)).astype(BF16)
    asked = jnp.dot(expand, ids[:, 0, :].astype(BF16), preferred_element_type=F32)
    row_c = iota((total, 1), 0)
    second = lax.rem(row_c // part, CAP) == 1
    wanted = jnp.where(second, asked[:, 1:2], asked[:, 0:1])
    offset = (lax.rem(row_c, part) + core * part).astype(F32)
    target = jnp.where(wanted < 0.0, -1e6, wanted * pair) + offset
    pick = (iota((total, blocks * pair), 1).astype(F32) == target).astype(BF16)
    outgoing[...] = jnp.dot(
        pick, rows_here[...].reshape(blocks * pair, width), preferred_element_type=F32
    ).astype(BF16).reshape(nd, pair, width)

    def send_rows(step, carry):
        peer = lax.rem(me + step, nd)
        pltpu.make_async_remote_copy(
            src_ref=outgoing.at[peer], dst_ref=arrived.at[me], send_sem=row_send, recv_sem=row_recv,
            device_id=(peer, hd), device_id_type=MESH,
        ).start()
        return carry

    lax.fori_loop(1, nd, send_rows, 0)
    own_rows = pltpu.make_async_copy(outgoing.at[me], arrived.at[me], local_sem.at[3])
    own_rows.start()

    spread = (iota((reqs * part, reqs), 0) // part == iota((reqs * part, reqs), 1)).astype(BF16)
    place = jnp.broadcast_to(rank_col * CAP + within_col, (reqs, 128)).astype(BF16)
    place = jnp.dot(spread, place, preferred_element_type=F32)[:, 0:1]
    place = place * part + lax.rem(iota((reqs * part, 1), 0), part).astype(F32)
    choose = (iota((reqs * part, total), 1).astype(F32) == place).astype(BF16)
    own_rows.wait()
    wait_bytes(arrived.at[pl.ds(0, nd - 1)], row_recv)
    chunk[...] = jnp.dot(
        choose, arrived[...].reshape(total, width), preferred_element_type=F32
    ).astype(BF16)

    def share(source, index, peer, slot):
        return pltpu.make_async_remote_copy(
            src_ref=source, dst_ref=keys_ref.at[index], send_sem=ag_send.at[slot],
            recv_sem=ag_recv.at[index], device_id=(me, peer), device_id_type=MESH,
        )

    chips = nh // 2
    for step in range(1, chips):
        share(chunk, hd, lax.rem(hd + 2 * step, nh), step).start()
    share(chunk, hd, sibling, 0).start()
    own_chunk = pltpu.make_async_copy(chunk, keys_ref.at[hd], local_sem.at[4])
    own_chunk.start()
    for step in range(1, chips):
        source = lax.rem(hd - 2 * step + nh, nh)
        share(chunk, source, sibling, 0).wait_recv()
        share(keys_ref.at[source], source, sibling, chips + step).start()
    for step in range(chips):
        source = lax.rem(sibling + 2 * step, nh)
        share(chunk, source, sibling, 0).wait_recv()

    own_chunk.wait()
    for step in range(chips):
        share(chunk, hd, sibling, step).wait_send()
    for step in range(1, chips):
        share(chunk, hd, sibling, chips + step).wait_send()
    own_q.wait()
    wait_bytes(qg_ref.at[pl.ds(0, (nh - 1) * q_rows)], q_recv)
    wait_bytes(qg_ref.at[pl.ds(0, (nh - 1) * q_rows)], q_send)
    wait_bytes(outgoing.at[pl.ds(0, nd - 1)], row_send)
    wait_bytes(table.at[pl.ds(0, nd - 1)], id_send)


def attend_kernel(
    qg_ref, latents_ref, cache_ref, keys_ref, key_up_ref, value_up_ref, start_ref, length_ref, out_ref,
    nope, rope, query_p, query_d, mixed_p, mixed_d, values, seen,
):
    rows, heads, q_width = qg_ref.shape
    nope_dim, latent = key_up_ref.shape[1], key_up_ref.shape[2]
    rope_dim = q_width - nope_dim
    dec = start_ref.shape[1]
    pre = rows - dec
    width = latent + rope_dim
    pool = cache_ref.shape[0]
    exponent = float(q_width) ** (-0.5) * math.log2(math.e)

    flat = qg_ref[...].reshape(rows * heads, q_width).astype(F32)
    nope[...] = flat[:, :nope_dim]
    rope[:, :rope_dim] = flat[:, nope_dim:]
    for h in range(heads):
        picked = nope[pl.ds(h, rows, stride=heads), :].astype(BF16)
        absorbed = jnp.dot(picked, key_up_ref[h], preferred_element_type=F32).astype(BF16)
        turned = rope[pl.ds(h, rows, stride=heads), :].astype(BF16)[:, :rope_dim]
        query_p[pl.ds(h * pre, pre), :latent] = absorbed[:pre]
        query_p[pl.ds(h * pre, pre), latent:] = turned[:pre]
        query_d[pl.ds(h * dec, dec), :latent] = absorbed[pre:]
        query_d[pl.ds(h * dec, dec), latent:] = turned[pre:]

    def scores(query, keys):
        return lax.dot_general(query, keys, (((1,), (1,)), ((), ())), preferred_element_type=F32)

    def mix(first, keys, second, local):
        peak = jnp.maximum(
            jnp.max(first, axis=1, keepdims=True), jnp.max(second, axis=1, keepdims=True)
        ) * exponent
        raised1 = jnp.exp2(first * exponent - peak)
        raised2 = jnp.exp2(second * exponent - peak)
        total = jnp.sum(raised1, axis=1, keepdims=True) + jnp.sum(raised2, axis=1, keepdims=True)
        mixed = jnp.dot(raised1.astype(BF16), keys[:, :latent], preferred_element_type=F32)
        mixed += jnp.dot(raised2.astype(BF16), local[:, :latent], preferred_element_type=F32)
        return (mixed / total).astype(BF16)

    size = 2 * pre

    def prefill_block(index, carry):
        at = pl.ds(pl.multiple_of(index * size, size), size)
        query = query_p[at, :]
        local = latents_ref[:pre, :]
        keys = keys_ref[...]
        first = scores(query, keys)
        second = scores(query, local)
        position = lax.rem(iota((size, pre), 0), pre)
        second = jnp.where(iota((size, pre), 1) <= position, second, HIDDEN)
        mixed_p[at, :] = mix(first, keys, second, local)
        return carry

    lax.fori_loop(0, heads * pre // size, prefill_block, 0)

    eye = iota((dec, dec), 0) == iota((dec, dec), 1)
    start = jnp.sum(jnp.where(eye, start_ref[...].astype(F32), 0.0), axis=1, keepdims=True)
    length = jnp.sum(jnp.where(eye, length_ref[...].astype(F32), 0.0), axis=1, keepdims=True)
    place = iota((dec, pool), 1).astype(F32) - start
    seen[...] = jnp.where((place >= 0.0) & (place < length), 0.0, HIDDEN)
    group = size // dec

    def decode_block(index, carry):
        at = pl.ds(pl.multiple_of(index * size, size), size)
        query = query_d[at, :]
        local = latents_ref[rows - pre:, :]
        cache = cache_ref[...]
        first = (scores(query, cache).reshape(group, dec, pool) + seen[...][None]).reshape(size, pool)
        second = scores(query, local)
        own = lax.rem(iota((size, pre), 0), dec) + (pre - dec)
        second = jnp.where(iota((size, pre), 1) == own, second, HIDDEN)
        mixed_d[at, :] = mix(first, cache, second, local)
        return carry

    lax.fori_loop(0, heads * dec // size, decode_block, 0)

    for h in range(heads):
        values[pl.ds(h, pre, stride=heads), :] = jnp.dot(
            mixed_p[pl.ds(h * pre, pre), :], value_up_ref[h], preferred_element_type=F32
        )
        values[pl.ds(pre * heads + h, dec, stride=heads), :] = jnp.dot(
            mixed_d[pl.ds(h * dec, dec), :], value_up_ref[h], preferred_element_type=F32
        )
    out_ref[...] = values[...].astype(BF16).reshape(out_ref.shape)


def return_kernel(values_ref, out_ref, local_sem, send_sem, recv_sem):
    nh = lax.axis_size("head")
    me, hd = lax.axis_index("dp"), lax.axis_index("head")
    heads = values_ref.shape[1]
    rows = out_ref.shape[0]
    barrier = pltpu.get_barrier_semaphore()

    def greet(step, carry):
        peer = lax.rem(hd + step, nh)
        pl.semaphore_signal(barrier, inc=1, device_id=(me, peer), device_id_type=MESH)
        return carry

    lax.fori_loop(1, nh, greet, 0)
    here = pl.ds(pl.multiple_of(hd * heads, heads), heads)
    own = pltpu.make_async_copy(values_ref.at[pl.ds(hd * rows, rows)], out_ref.at[:, here, :], local_sem)
    own.start()
    pl.semaphore_wait(barrier, nh - 1)

    def send(step, carry):
        peer = lax.rem(hd + step, nh)
        pltpu.make_async_remote_copy(
            src_ref=values_ref.at[pl.ds(peer * rows, rows)], dst_ref=out_ref.at[:, here, :],
            send_sem=send_sem, recv_sem=recv_sem, device_id=(me, peer), device_id_type=MESH,
        ).start()
        return carry

    lax.fori_loop(1, nh, send, 0)
    own.wait()
    wait_bytes(values_ref.at[pl.ds(0, (nh - 1) * rows)], send_sem)
    wait_bytes(values_ref.at[pl.ds(0, (nh - 1) * rows)], recv_sem)


def body(
    queries, latents, cache_pool, key_up, value_up, prefix_rank, prefix_block, decode_start, decode_length
):
    nd, nh = lax.axis_size("dp"), lax.axis_size("head")
    q_rows, all_heads, q_width = queries.shape
    heads = all_heads // nh
    rows = q_rows * nh
    blocks, block_rows, width = cache_pool.shape
    part = block_rows // nh
    pair = CAP * part
    reqs = prefix_block.shape[0]
    latent = key_up.shape[2]
    dec = decode_start.shape[0]
    pre = rows - dec
    v_dim = value_up.shape[2]
    anywhere = pl.BlockSpec(memory_space=pl.ANY)
    vmem = pl.BlockSpec(memory_space=pltpu.VMEM)
    dma = pltpu.SemaphoreType.DMA

    grouped, keys = pl.pallas_call(
        gather_kernel,
        out_shape=[
            jax.ShapeDtypeStruct((rows, heads, q_width), BF16),
            jax.ShapeDtypeStruct((nh, reqs * part, width), BF16),
        ],
        in_specs=[anywhere, anywhere, vmem, vmem],
        out_specs=[anywhere, anywhere],
        scratch_shapes=[
            pltpu.VMEM((nd, 1, 128), F32),
            pltpu.VMEM((nd, 1, 128), F32),
            pltpu.VMEM((blocks, pair, width), BF16),
            pltpu.VMEM((nd, pair, width), BF16),
            pltpu.VMEM((nd, pair, width), BF16),
            pltpu.VMEM((reqs * part, width), BF16),
            dma((5,)), dma, dma, dma, dma, dma, dma, dma((nh,)), dma((nh,)),
        ],
        compiler_params=pltpu.CompilerParams(
            collective_id=0, has_side_effects=True, vmem_limit_bytes=32 * 2**20
        ),
        name="gather",
    )(queries, cache_pool, prefix_rank, prefix_block.reshape(1, reqs))

    values = pl.pallas_call(
        attend_kernel,
        out_shape=jax.ShapeDtypeStruct((rows, heads, v_dim), BF16),
        in_specs=[vmem] * 8,
        out_specs=vmem,
        scratch_shapes=[
            pltpu.VMEM((rows * heads, 128), F32),
            pltpu.VMEM((rows * heads, 128), F32),
            pltpu.VMEM((pre * heads, width), BF16),
            pltpu.VMEM((dec * heads, width), BF16),
            pltpu.VMEM((pre * heads, latent), BF16),
            pltpu.VMEM((dec * heads, latent), BF16),
            pltpu.VMEM((rows * heads, v_dim), F32),
            pltpu.VMEM((dec, blocks * block_rows), F32),
        ],
        compiler_params=pltpu.CompilerParams(vmem_limit_bytes=56 * 2**20),
        name="attend",
    )(
        grouped, latents, cache_pool.reshape(blocks * block_rows, width),
        keys.reshape(nh * reqs * part, width), key_up, value_up,
        decode_start.reshape(1, dec), decode_length.reshape(1, dec),
    )

    return pl.pallas_call(
        return_kernel,
        out_shape=jax.ShapeDtypeStruct((q_rows, all_heads, v_dim), BF16),
        in_specs=[anywhere],
        out_specs=anywhere,
        scratch_shapes=[dma, dma, dma],
        compiler_params=pltpu.CompilerParams(collective_id=1, has_side_effects=True),
        name="give_back",
    )(values)


def solution(mesh):
    return jax.shard_map(
        body,
        mesh=mesh,
        in_specs=(
            P(("dp", "head"), None, None),
            P("dp", None),
            P("dp", None, None),
            P("head", None, None),
            P("head", None, None),
            P("dp", None),
            P("dp"),
            P("dp"),
            P("dp"),
        ),
        out_specs=P(("dp", "head"), None, None),
        check_vma=False,
    )
```

time: 245 us -> 111 us (0.45); the launches traced: 241 us -> 111 us
  waiting for transfers between devices: 112 us -> 0 us
  Pallas kernels: 0 us -> 103 us
  matrix products: 39 us -> 0 us
  local copies, waits for them, and re-layouts: 36.9 us -> 8.56 us
  starting transfers between devices: 23.6 us -> 0 us
  blocking collectives: 16.1 us -> 0 us
  other arithmetic: 13.4 us -> 0 us
    all_to_all x3 -> x0, waiting for transfers between devices: 112 us -> none  [the longest x1 90.9 us: body(): lax.all_to_all(outgoing, 'dp', split_axis=0, concat_axis=0, tiled=True)]
    pallas_call x0 -> x3, Pallas kernels: none -> 103 us  [the longest x1 50.7 us: body(): pl.pallas_call(gather_kernel, out_shape=[jax.ShapeDtypeStruct((rows, head...]
    dot_general x21 -> x0, matrix products: 39 us -> none  [the longest x4 15.5 us: prefill_block(): jnp.einsum('qd,kd->qk', block_query, prefix_keys, preferred_element_type=...]
    all_to_all x3 -> x0, starting transfers between devices: 23.6 us -> none  [the longest x1 11.9 us: body(): lax.all_to_all(wanted, 'dp', split_axis=0, concat_axis=0, tiled=True)]
    all_to_all x1 -> x0, blocking collectives: 16.1 us -> none  [body(): lax.all_to_all(head_values, 'head', split_axis=0, concat_axis=1, tiled=True)]
    gather x2 -> x0, local copies, waits for them, and re-layouts: 10.1 us -> none  [the longest x1 5.27 us: body(): outgoing = cache_pool[safe_ids]]
    reduce_sum x11 -> x0, other arithmetic: 5.33 us -> none  [the longest x4 3.27 us: two_part_mix(): jnp.sum(raised_first, axis=1, keepdims=True)]
    slice x6 -> x0, local copies, waits for them, and re-layouts: 4.29 us -> none  [the longest x1 3.02 us: body(): query_cat[:prefill_rows].reshape(block_count, block_size, width_all)]
  transfers between devices with their start and end apart: 3 -> 0, of which waited for: 3 -> 0; matrix products, arithmetic and copies ran while one was open for 13% -> 0% of each run, Pallas kernels for 0% -> 0%
where the time goes in v1:
time: 111 us
  Pallas kernels  103 us (93%)
  local copies, waits for them, and re-layouts  8.56 us (8%)
    pallas_call x1, Pallas kernels, body(): pl.pallas_call(gather_kernel, out_shape=[jax.ShapeDtypeStruct((rows, head...  50.7 us
    pallas_call x1, Pallas kernels, body(): pl.pallas_call(attend_kernel, out_shape=jax.ShapeDtypeStruct((rows, heads...  40.6 us
    pallas_call x1, Pallas kernels, body(): pl.pallas_call(return_kernel, out_shape=jax.ShapeDtypeStruct((q_rows, all...  11.4 us
    unnamed x11, local copies, waits for them, and re-layouts  8.56 us

profile of v1, /device:TPU:1, one launch (start us, length us, event | category | flops | bytes accessed | tf_op | source)
XLA Modules:
  0.0 111.2 jit_solution(2367928013954319400)
XLA Ops:
  0.0 0.0 copy-start.3
  0.0 0.7 copy.11.rank_ref
  0.8 1.5 %copy.10.q_ref = bf16[20,128,192]{2,1,0:T(8,128)(2,1)S(1)} copy(bf16[20,128,192]{1,2,0:T(8,128)(2,1)} %param.9) | data formatting | bytes 1966080 | tf_op args[0]
  2.3 0.0 copy-done.3
  2.3 0.0 copy-start
  2.3 1.7 %copy-done = bf16[32,64,576]{2,1,0:T(8,128)(2,1)S(1)} copy-done((bf16[32,64,576]{2,1,0:T(8,128)(2,1)S(1)}, bf16[32,64,576]{2,1,0:T(8,128)(2,1)}, u32[]{:S(2)}) %copy-start) | copy-done | bytes 2359320
  4.1 50.7 %gather.1 = (bf16[160,16,192]{2,1,0:T(8,128)(2,1)S(1)}, bf16[8,256,576]{2,1,0:T(8,128)(2,1)S(1)}) custom-call(bf16[20,128,192]{2,1,0:T(8,128)(2,1)S(1)} %copy.10.q_ref, bf16[32,64,576]{2,1,0:T(8,128)(2,1)S(1)} %copy-done, s32[32,1]{1,0:T(8,128)S(1)} %copy.11.rank_ref, s32[1,32]{1,0:T(1,128)S(1)} %bitcast.7), custom_call_target="tpu_custom_call" | custom-call | tf_op jit(solution)/shard_map/gather/pallas_call | solution.py:312
  54.7 0.0 copy-start.1
  54.7 1.5 %copy-done.1 = bf16[8,256,576]{2,1,0:T(8,128)(2,1)} copy-done((bf16[8,256,576]{2,1,0:T(8,128)(2,1)}, bf16[8,256,576]{2,1,0:T(8,128)(2,1)S(1)}, u32[]{:S(2)}) %copy-start.1) | copy-done | bytes 2359320
  56.2 0.0 copy-start.2
  56.2 1.1 copy-done.2
  57.3 40.6 %attend.1.values_ref = bf16[160,16,128]{2,1,0:T(8,128)(2,1)} custom-call(bf16[160,16,192]{2,1,0:T(8,128)(2,1)} %copy-done.2, bf16[160,576]{1,0:T(8,128)(2,1)} %latents_ref.1, bf16[2048,576]{1,0:T(8,128)(2,1)} %bitcast.5, bf16[2048,576]{1,0:T(8,128)(2,1)} %bitcast.6, bf16[16,128,512]{2,1,0:T(8,128)(2,1)} %key_up_ref.1, bf16[16,512,128]{2,1,0:T(8,128)(2,1)} %value_up_ref.1, ...), custom_call_target="tpu_custom_call" | custom-call | tf_op jit(solution)/shard_map/attend/pallas_call | solution.py:335
  97.9 11.4 %give_back.1 = bf16[20,128,128]{2,1,0:T(8,128)(2,1)} custom-call(bf16[160,16,128]{2,1,0:T(8,128)(2,1)} %attend.1.values_ref), custom_call_target="tpu_custom_call" | custom-call | tf_op jit(solution)/shard_map/give_back/pallas_call | solution.py:358
  109.3 2.0 %copy.13 = bf16[20,128,128]{2,1,0:T(8,128)(2,1)} copy(bf16[20,128,128]{2,1,0:T(8,128)(2,1)} %give_back.1) | data formatting | bytes 1310720
Async XLA Ops:
  0.0 2.3 %copy-start.3 = (s32[32]{0:T(128)S(1)}, s32[32]{0:T(128)}, u32[]{:S(2)}) copy-start(s32[32]{0:T(128)} %param.15) | copy-start | bytes 388
  2.3 1.7 %copy-start = (bf16[32,64,576]{2,1,0:T(8,128)(2,1)S(1)}, bf16[32,64,576]{2,1,0:T(8,128)(2,1)}, u32[]{:S(2)}) copy-start(bf16[32,64,576]{2,1,0:T(8,128)(2,1)} %cache_ref.1) | copy-start | bytes 7077892
  54.7 1.5 %copy-start.1 = (bf16[8,256,576]{2,1,0:T(8,128)(2,1)}, bf16[8,256,576]{2,1,0:T(8,128)(2,1)S(1)}, u32[]{:S(2)}) copy-start(bf16[8,256,576]{2,1,0:T(8,128)(2,1)S(1)} %get-tuple-element.8) | copy-start | bytes 7077892
  56.2 1.1 copy-start.2

commit v2 on v0

v2 whole, which is shorter than its diff:
```python
import functools
import math

import jax
import jax.numpy as jnp
from jax import lax
from jax.experimental import pallas as pl
from jax.experimental.pallas import tpu as pltpu
from jax.sharding import PartitionSpec as P

MESH = pl.DeviceIdType.MESH
CAP = 2
F32 = jnp.float32
BF16 = jnp.bfloat16
HIDDEN = -1e30


def iota(shape, dim):
    return lax.broadcasted_iota(jnp.int32, shape, dim)


def wait_bytes(ref, sem):
    pltpu.make_async_copy(ref, ref, sem).wait()


def gather_lists(rank_row, block_row, nd):
    reqs = rank_row.shape[1]
    half = reqs // 2
    row_i, col_i = iota((reqs, reqs), 0), iota((reqs, reqs), 1)

    def down(mask, values=1.0):
        return jnp.sum(jnp.where(mask, values, 0.0), axis=0, keepdims=True)

    def across(mask, values=1.0):
        return jnp.sum(jnp.where(mask, values, 0.0), axis=1, keepdims=True)

    rank_col = across(row_i == col_i, rank_row)
    same = rank_col == rank_row
    slot_row = down(same & (row_i < col_i))
    slot_col = across(same & (col_i < row_i))
    hit = rank_row == iota((nd, reqs), 0).astype(F32)
    want0 = across(hit & (slot_row == 0.0), block_row + 1.0) - 1.0
    want1 = across(hit & (slot_row == 1.0), block_row + 1.0) - 1.0
    spot_row = down((row_i < col_i) & (slot_col == 0.0))
    spot_col = across((col_i < row_i) & (slot_row == 0.0))
    early_row = (slot_row == 0.0) & (spot_row < half)
    early_col = (slot_col == 0.0) & (spot_col < half)
    late_row = down((row_i < col_i) & jnp.logical_not(early_col))
    order = iota((half, reqs), 0).astype(F32)
    early = across((order == spot_row) & early_row, rank_row)
    late = across((order == late_row) & jnp.logical_not(early_row), slot_row * nd + rank_row)
    return want0, want1, early, late


def spread_rows(column, part):
    count = column.shape[0]
    expand = (iota((count * part, count), 0) // part == iota((count * part, count), 1)).astype(BF16)
    wide = jnp.broadcast_to(column, (count, 128)).astype(BF16)
    spread = jnp.dot(expand, wide, preferred_element_type=F32)[:, 0:1]
    return spread * part + lax.rem(iota((count * part, 1), 0), part).astype(F32)


def pick_rows(target, first, source):
    total = source.shape[0]
    pick = (iota((target.shape[0], total), 1).astype(F32) + first == target).astype(BF16)
    return jnp.dot(pick, source, preferred_element_type=F32)


def scores(query, keys):
    return lax.dot_general(query, keys, (((1,), (1,)), ((), ())), preferred_element_type=F32)


def kernel(
    q_ref, latents_hbm, cache_hbm, key_up_hbm, value_up_hbm, rank_ref, block_ref, start_ref, length_ref,
    out_ref,
    q_in, latents, cache, key_up, value_up, rows_here, table, ids,
    nope_out, rope_out, nope_in, rope_in, nope, rope, out0, out1, in0, in1, keys_a, keys_b,
    query_p, query_d, mixed_p, mixed_d, values, values_out, seen, acc, peak, total,
    local_sem, id_send, id_recv, nope_send, nope_recv, rope_send, rope_recv,
    send0, recv0, send1, recv1, a_send, a_recv, b_send, b_recv, out_send, out_recv, own_sem,
):
    nd, nh = lax.axis_size("dp"), lax.axis_size("head")
    chips = nh // 2
    me, hd = lax.axis_index("dp"), lax.axis_index("head")
    chip, core = hd // 2, hd % 2
    sibling = chip * 2 + 1 - core
    blocks, block_rows, width = cache_hbm.shape
    part = block_rows // nh
    pair = CAP * part
    q_rows, q_width, all_heads = q_ref.shape
    heads, nope_dim, latent = key_up_hbm.shape
    rope_dim = q_width - nope_dim
    rows = q_rows * nh
    reqs = rank_ref.shape[1]
    dec = start_ref.shape[1]
    pre = rows - dec
    pool = blocks * block_rows
    exponent = float(q_width) ** (-0.5) * math.log2(math.e)
    front = chips - 1

    def place_of(device):
        moved = jnp.where(device % 2 == 0, device // 2, front + device // 2)
        return jnp.where(device < 2 * front, moved, device) * q_rows

    loads = [
        pltpu.make_async_copy(source, dest, local_sem.at[i])
        for i, (source, dest) in enumerate([
            (q_ref, q_in),
            (cache_hbm.at[:, pl.ds(pl.multiple_of(chip * pair, pair), pair), :], rows_here),
            (key_up_hbm, key_up), (latents_hbm, latents), (cache_hbm, cache), (value_up_hbm, value_up),
        ])
    ]
    for load in loads:
        load.start()
    barrier = pltpu.get_barrier_semaphore()

    def greet_dp(step, carry):
        pl.semaphore_signal(barrier, inc=1, device_id=(lax.rem(me + step, nd), hd), device_id_type=MESH)
        return carry

    def greet_head(step, carry):
        pl.semaphore_signal(barrier, inc=1, device_id=(me, lax.rem(hd + step, nh)), device_id_type=MESH)
        return carry

    lax.fori_loop(1, nd, greet_dp, 0)
    lax.fori_loop(1, nh, greet_head, 0)

    want0, want1, early, late = gather_lists(
        rank_ref[...].astype(F32), block_ref[...].astype(F32), nd
    )
    lane = iota((nd, 128), 1)
    table[:, 0, :] = jnp.where(lane == 0, want0, jnp.where(lane == 1, want1, 0.0))

    pl.semaphore_wait(barrier, nd - 1 + nh - 1)

    def send_ids(step, carry):
        peer = lax.rem(me + step, nd)
        pltpu.make_async_remote_copy(
            src_ref=table.at[peer], dst_ref=ids.at[me], send_sem=id_send, recv_sem=id_recv,
            device_id=(peer, hd), device_id_type=MESH,
        ).start()
        return carry

    lax.fori_loop(1, nd, send_ids, 0)
    own_ids = pltpu.make_async_copy(table.at[me], ids.at[me], own_sem.at[0])
    own_ids.start()

    loads[0].wait()
    half_heads = heads // 2

    def turn(step, carry):
        turned = []
        for k in range(2):
            one = jnp.transpose(q_in[2 * step + k].astype(F32), (1, 0))
            nope_out[2 * step + k] = one[:, :nope_dim].astype(BF16)
            both = one[:, nope_dim:].reshape(nh, 2, half_heads, rope_dim)
            turned.append(jnp.concatenate([both[:, 0], both[:, 1]], axis=2))
        at = pl.ds(pl.multiple_of(step * 2 * half_heads, 2 * half_heads), 2 * half_heads)
        rope_out[:, at, :] = jnp.concatenate(turned, axis=1).astype(BF16)
        return carry

    lax.fori_loop(0, q_rows // 2, turn, 0)

    here = place_of(hd)

    def q_copies(peer, remote):
        nope_from = nope_out.at[:, pl.ds(pl.multiple_of(peer * heads, heads), heads), :]
        nope_to = nope_in.at[pl.ds(here, q_rows)]
        rope_to = rope_in.at[here // q_rows]
        if not remote:
            return [
                pltpu.make_async_copy(nope_from, nope_to, own_sem.at[1]),
                pltpu.make_async_copy(rope_out.at[peer], rope_to, own_sem.at[2]),
            ]
        return [
            pltpu.make_async_remote_copy(
                src_ref=nope_from, dst_ref=nope_to, send_sem=nope_send, recv_sem=nope_recv,
                device_id=(me, peer), device_id_type=MESH,
            ),
            pltpu.make_async_remote_copy(
                src_ref=rope_out.at[peer], dst_ref=rope_to, send_sem=rope_send, recv_sem=rope_recv,
                device_id=(me, peer), device_id_type=MESH,
            ),
        ]

    def send_q(step, carry):
        for copy in q_copies(lax.rem(hd + step, nh), True):
            copy.start()
        return carry

    lax.fori_loop(1, nh, send_q, 0)
    own_q = q_copies(hd, False)
    for copy in own_q:
        copy.start()

    loads[1].wait()
    own_ids.wait()
    wait_bytes(ids.at[pl.ds(0, nd - 1)], id_recv)
    expand = (iota((nd * part, nd), 0) // part == iota((nd * part, nd), 1)).astype(BF16)
    asked = jnp.dot(expand, ids[:, 0, :].astype(BF16), preferred_element_type=F32)
    offset = (lax.rem(iota((nd * part, 1), 0), part) + core * part).astype(F32)

    def row_copy(source, dest, send_sem, recv_sem, peer):
        return pltpu.make_async_remote_copy(
            src_ref=source.at[peer], dst_ref=dest.at[me], send_sem=send_sem, recv_sem=recv_sem,
            device_id=(peer, hd), device_id_type=MESH,
        )

    own_rows = []
    for slot, (source, dest, send_sem, recv_sem) in enumerate(
        [(out0, in0, send0, recv0), (out1, in1, send1, recv1)]
    ):
        wanted = asked[:, slot:slot + 1]
        target = jnp.where(wanted < 0.0, -1e6, wanted * pair) + offset
        picked = pick_rows(target, 0.0, rows_here[...].reshape(blocks * pair, width))
        source[...] = picked.astype(BF16).reshape(nd, part, width)

        def send_rows(step, carry, source=source, dest=dest, send_sem=send_sem, recv_sem=recv_sem):
            row_copy(source, dest, send_sem, recv_sem, lax.rem(me + step, nd)).start()
            return carry

        lax.fori_loop(1, nd, send_rows, 0)
        own = pltpu.make_async_copy(source.at[me], dest.at[me], own_sem.at[3 + slot])
        own.start()
        own_rows.append(own)

    for copy in own_q:
        copy.wait()
    loads[2].wait()
    wait_bytes(nope_in.at[pl.ds(0, rows - q_rows)], nope_recv)
    wait_bytes(rope_in.at[pl.ds(0, nh - 1)], rope_recv)
    nope[...] = nope_in[...].reshape(rows * heads, nope_dim).astype(F32)
    rope[...] = rope_in[...].reshape(rows * half_heads, 2 * rope_dim).astype(F32)
    part_rows = pre // 2

    def put_query(h, columns, value):
        for side in range(2):
            at = pl.ds((side * heads + h) * part_rows, part_rows)
            query_p[at, columns] = value[side * part_rows:(side + 1) * part_rows]
        query_d[pl.ds(h * dec, dec), columns] = value[pre:]

    for h in range(heads):
        picked = nope[pl.ds(h, rows, stride=heads), :].astype(BF16)
        absorbed = jnp.dot(picked, key_up[h], preferred_element_type=F32).astype(BF16)
        put_query(h, slice(0, latent), absorbed)
    for h in range(half_heads):
        both = rope[pl.ds(h, rows, stride=half_heads), :].astype(BF16)
        put_query(h, slice(latent, width), both[:, :rope_dim])
        put_query(h + half_heads, slice(latent, width), both[:, rope_dim:])

    def share(keys, send_sem, recv_sem, index, peer, slot):
        return pltpu.make_async_remote_copy(
            src_ref=keys.at[index], dst_ref=keys.at[index], send_sem=send_sem.at[slot],
            recv_sem=recv_sem.at[index], device_id=(me, peer), device_id_type=MESH,
        )

    def share_own(*gang):
        for step in range(1, chips):
            share(*gang, hd, lax.rem(hd + 2 * step, nh), step).start()
        share(*gang, hd, sibling, 0).start()

    def share_on(*gang):
        for step in range(1, chips):
            source = lax.rem(hd - 2 * step + nh, nh)
            share(*gang, source, sibling, 0).wait_recv()
            share(*gang, source, sibling, chips + step).start()

    def share_end(*gang):
        for step in range(chips):
            share(*gang, lax.rem(sibling + 2 * step, nh), sibling, 0).wait_recv()

    def share_sent(*gang):
        for slot in [*range(chips), *range(chips + 1, 2 * chips)]:
            share(*gang, hd, sibling, slot).wait_send()

    gang_a = (keys_a, a_send, a_recv)
    gang_b = (keys_b, b_send, b_recv)

    own_rows[0].wait()
    wait_bytes(in0.at[pl.ds(0, nd - 1)], recv0)
    first_rows = in0[...].reshape(nd * part, width)
    keys_a[hd] = pick_rows(spread_rows(early, part), 0.0, first_rows).astype(BF16)
    share_own(*gang_a)

    loads[3].wait()
    loads[4].wait()
    eye = iota((dec, dec), 0) == iota((dec, dec), 1)
    start = jnp.sum(jnp.where(eye, start_ref[...].astype(F32), 0.0), axis=1, keepdims=True)
    length = jnp.sum(jnp.where(eye, length_ref[...].astype(F32), 0.0), axis=1, keepdims=True)
    place = iota((dec, pool), 1).astype(F32) - start
    seen[...] = jnp.where((place >= 0.0) & (place < length), 0.0, HIDDEN)
    step_blocks = blocks // 4
    step_keys = step_blocks * block_rows
    size_d = heads * dec // 2

    def decode_block(index, carry):
        at = pl.ds(pl.multiple_of(index * size_d, size_d), size_d)
        query = query_d[at, :]
        local = latents[rows - pre:, :]
        own = lax.rem(iota((size_d, pre), 0), dec) + (pre - dec)
        kept = [jnp.where(iota((size_d, pre), 1) == own, scores(query, local), HIDDEN)]
        held = [local]
        for j in range(4):
            keys = cache[j * step_blocks:(j + 1) * step_blocks].reshape(step_keys, width)
            one = scores(query, keys).reshape(size_d // dec, dec, step_keys)
            one = one + seen[:, j * step_keys:(j + 1) * step_keys][None]
            kept.append(one.reshape(size_d, step_keys))
            held.append(keys)
        top = functools.reduce(jnp.maximum, [jnp.max(x, axis=1, keepdims=True) for x in kept]) * exponent
        weight, mixed = 0.0, 0.0
        for x, keys in zip(kept, held):
            raised = jnp.exp2(x * exponent - top)
            weight += jnp.sum(raised, axis=1, keepdims=True)
            mixed += jnp.dot(raised.astype(BF16), keys[:, :latent], preferred_element_type=F32)
        mixed_d[at, :] = (mixed / weight).astype(BF16)
        return carry

    lax.fori_loop(0, 2, decode_block, 0)
    share_on(*gang_a)

    def give(device):
        source = values_out.at[pl.ds(pl.multiple_of(place_of(jnp.int32(device)), 4), q_rows)]
        dest = out_ref.at[:, pl.ds(pl.multiple_of(hd * heads, heads), heads), :]

        @pl.when(hd != device)
        def _():
            pltpu.make_async_remote_copy(
                src_ref=source, dst_ref=dest, send_sem=out_send, recv_sem=out_recv,
                device_id=(me, device), device_id_type=MESH,
            ).start()

        @pl.when(hd == device)
        def _():
            pltpu.make_async_copy(source, dest, own_sem.at[5]).start()

    def put_values(first, count, mixed, base):
        for h in range(heads):
            values[pl.ds(first * heads + h, count, stride=heads), :] = jnp.dot(
                mixed[pl.ds(base + h * count, count), :], value_up[h], preferred_element_type=F32
            )
        done = values[pl.ds(first * heads, count * heads), :].astype(BF16)
        values_out[pl.ds(first, count)] = done.reshape(count, heads, done.shape[1])

    loads[5].wait()
    put_values(pre, dec, mixed_d, 0)
    give(nh - 1)

    share_end(*gang_a)
    own_rows[1].wait()
    wait_bytes(in1.at[pl.ds(0, nd - 1)], recv1)
    target = spread_rows(late, part)
    keys_b[hd] = (
        pick_rows(target, 0.0, in0[...].reshape(nd * part, width))
        + pick_rows(target, float(nd * part), in1[...].reshape(nd * part, width))
    ).astype(BF16)
    share_own(*gang_b)

    size = heads * part_rows // 2
    key_count = reqs // 2 * block_rows

    def early_block(index, carry):
        at = pl.ds(pl.multiple_of(index * size, size), size)
        query = query_p[at, :]
        local = latents[:pre, :]
        keys = keys_a[...].reshape(key_count, width)
        row = lax.rem(iota((size, pre), 0), part_rows) + (index // 2) * part_rows
        group = row // q_rows
        moved = jnp.where(group < front, 2 * group, 2 * (group - front) + 1) - group
        row = jnp.where(group < 2 * front, row + moved * q_rows, row)
        second = jnp.where(iota((size, pre), 1) <= row, scores(query, local), HIDDEN)
        first = scores(query, keys)
        top = jnp.maximum(
            jnp.max(first, axis=1, keepdims=True), jnp.max(second, axis=1, keepdims=True)
        ) * exponent
        raised1 = jnp.exp2(first * exponent - top)
        raised2 = jnp.exp2(second * exponent - top)
        weight = jnp.sum(raised1, axis=1, keepdims=True) + jnp.sum(raised2, axis=1, keepdims=True)
        mixed = jnp.dot(raised1.astype(BF16), keys[:, :latent], preferred_element_type=F32)
        mixed += jnp.dot(raised2.astype(BF16), local[:, :latent], preferred_element_type=F32)
        acc[at, :] = mixed
        peak[at, :] = jnp.broadcast_to(top, (size, 128))
        total[at, :] = jnp.broadcast_to(weight, (size, 128))
        return carry

    def late_block(index, carry):
        at = pl.ds(pl.multiple_of(index * size, size), size)
        keys = keys_b[...].reshape(key_count, width)
        first = scores(query_p[at, :], keys)
        old = peak[at, :][:, 0:1]
        top = jnp.maximum(old, jnp.max(first, axis=1, keepdims=True) * exponent)
        fix = jnp.exp2(old - top)
        raised = jnp.exp2(first * exponent - top)
        weight = total[at, :][:, 0:1] * fix + jnp.sum(raised, axis=1, keepdims=True)
        mixed = acc[at, :] * fix
        mixed += jnp.dot(raised.astype(BF16), keys[:, :latent], preferred_element_type=F32)
        mixed_p[at, :] = (mixed / weight).astype(BF16)
        return carry

    lax.fori_loop(0, 2, early_block, 0)
    share_on(*gang_b)
    lax.fori_loop(2, 4, early_block, 0)
    share_end(*gang_b)
    lax.fori_loop(0, 2, late_block, 0)
    put_values(0, part_rows, mixed_p, 0)
    for device in range(0, 2 * front, 2):
        give(device)
    lax.fori_loop(2, 4, late_block, 0)
    put_values(part_rows, part_rows, mixed_p, heads * part_rows)
    for device in [*range(1, 2 * front, 2), *range(2 * front, nh - 1)]:
        give(device)

    share_sent(*gang_a)
    share_sent(*gang_b)
    wait_bytes(nope_in.at[pl.ds(0, rows - q_rows)], nope_send)
    wait_bytes(rope_in.at[pl.ds(0, nh - 1)], rope_send)
    wait_bytes(in0.at[pl.ds(0, nd - 1)], send0)
    wait_bytes(in1.at[pl.ds(0, nd - 1)], send1)
    wait_bytes(table.at[pl.ds(0, nd - 1)], id_send)
    wait_bytes(values_out.at[pl.ds(0, q_rows)], own_sem.at[5])
    wait_bytes(values_out.at[pl.ds(0, rows - q_rows)], out_send)
    wait_bytes(values_out.at[pl.ds(0, rows - q_rows)], out_recv)


def body(
    queries, latents, cache_pool, key_up, value_up, prefix_rank, prefix_block, decode_start, decode_length
):
    nd, nh = lax.axis_size("dp"), lax.axis_size("head")
    q_rows, all_heads, q_width = queries.shape
    heads, nope_dim, latent = key_up.shape
    rows = q_rows * nh
    blocks, block_rows, width = cache_pool.shape
    part = block_rows // nh
    pair = CAP * part
    reqs = prefix_block.shape[0]
    dec = decode_start.shape[0]
    pre = rows - dec
    v_dim = value_up.shape[2]
    anywhere = pl.BlockSpec(memory_space=pl.ANY)
    vmem = pl.BlockSpec(memory_space=pltpu.VMEM)
    dma = pltpu.SemaphoreType.DMA
    half_keys = (nh, reqs // 2 * part, width)
    half_heads = heads // 2
    buffers = [
        ((q_rows, q_width, all_heads), BF16),
        (latents.shape, BF16),
        (cache_pool.shape, BF16),
        (key_up.shape, BF16),
        (value_up.shape, BF16),
        ((blocks, pair, width), BF16),
        ((nd, 1, 128), F32),
        ((nd, 1, 128), F32),
        ((q_rows, all_heads, nope_dim), BF16),
        ((nh, q_rows * half_heads, 2 * (q_width - nope_dim)), BF16),
        ((rows, heads, nope_dim), BF16),
        ((nh, q_rows * half_heads, 2 * (q_width - nope_dim)), BF16),
        ((rows * heads, nope_dim), F32),
        ((rows * half_heads, 2 * (q_width - nope_dim)), F32),
        ((nd, part, width), BF16),
        ((nd, part, width), BF16),
        ((nd, part, width), BF16),
        ((nd, part, width), BF16),
        (half_keys, BF16),
        (half_keys, BF16),
        ((pre * heads, width), BF16),
        ((dec * heads, width), BF16),
        ((pre * heads, latent), BF16),
        ((dec * heads, latent), BF16),
        ((rows * heads, v_dim), F32),
        ((rows, heads, v_dim), BF16),
        ((dec, blocks * block_rows), F32),
        ((pre * heads, latent), F32),
        ((pre * heads, 128), F32),
        ((pre * heads, 128), F32),
    ]
    return pl.pallas_call(
        kernel,
        out_shape=jax.ShapeDtypeStruct((q_rows, all_heads, v_dim), BF16),
        in_specs=[anywhere] * 5 + [vmem] * 4,
        out_specs=anywhere,
        scratch_shapes=[pltpu.VMEM(shape, dtype) for shape, dtype in buffers]
        + [dma((6,))] + [dma] * 10 + [dma((nh,))] * 4 + [dma, dma, dma((6,))],
        compiler_params=pltpu.CompilerParams(
            collective_id=0, has_side_effects=True, vmem_limit_bytes=60 * 2**20
        ),
        name="serve",
    )(
        jnp.swapaxes(queries, 1, 2), latents, cache_pool, key_up, value_up,
        prefix_rank.reshape(1, reqs), prefix_block.reshape(1, reqs),
        decode_start.reshape(1, dec), decode_length.reshape(1, dec),
    )


def solution(mesh):
    return jax.shard_map(
        body,
        mesh=mesh,
        in_specs=(
            P(("dp", "head"), None, None),
            P("dp", None),
            P("dp", None, None),
            P("head", None, None),
            P("head", None, None),
            P("dp", None),
            P("dp"),
            P("dp"),
            P("dp"),
        ),
        out_specs=P(("dp", "head"), None, None),
        check_vma=False,
    )
```

time: 245 us -> 75 us (0.31); the launches traced: 241 us -> 74.9 us
  waiting for transfers between devices: 112 us -> 0 us
  Pallas kernels: 0 us -> 72.9 us
  matrix products: 39 us -> 0 us
  local copies, waits for them, and re-layouts: 36.9 us -> 1.99 us
  starting transfers between devices: 23.6 us -> 0 us
  blocking collectives: 16.1 us -> 0 us
  other arithmetic: 13.4 us -> 0 us
    all_to_all x3 -> x0, waiting for transfers between devices: 112 us -> none  [the longest x1 90.9 us: body(): lax.all_to_all(outgoing, 'dp', split_axis=0, concat_axis=0, tiled=True)]
    pallas_call x0 -> x1, Pallas kernels: none -> 72.9 us  [body(): pl.pallas_call(kernel, out_shape=jax.ShapeDtypeStruct((q_rows, all_heads,...]
    dot_general x21 -> x0, matrix products: 39 us -> none  [the longest x4 15.5 us: prefill_block(): jnp.einsum('qd,kd->qk', block_query, prefix_keys, preferred_element_type=...]
    all_to_all x3 -> x0, starting transfers between devices: 23.6 us -> none  [the longest x1 11.9 us: body(): lax.all_to_all(wanted, 'dp', split_axis=0, concat_axis=0, tiled=True)]
    all_to_all x1 -> x0, blocking collectives: 16.1 us -> none  [body(): lax.all_to_all(head_values, 'head', split_axis=0, concat_axis=1, tiled=True)]
    gather x2 -> x0, local copies, waits for them, and re-layouts: 10.1 us -> none  [the longest x1 5.27 us: body(): outgoing = cache_pool[safe_ids]]
    reduce_sum x11 -> x0, other arithmetic: 5.33 us -> none  [the longest x4 3.27 us: two_part_mix(): jnp.sum(raised_first, axis=1, keepdims=True)]
    slice x6 -> x0, local copies, waits for them, and re-layouts: 4.29 us -> none  [the longest x1 3.02 us: body(): query_cat[:prefill_rows].reshape(block_count, block_size, width_all)]
  transfers between devices with their start and end apart: 3 -> 0, of which waited for: 3 -> 0; matrix products, arithmetic and copies ran while one was open for 13% -> 0% of each run, Pallas kernels for 0% -> 0%
where the time goes in v2:
time: 75 us; the launch traced here: 74.9 us
  Pallas kernels  72.9 us (97%)
  local copies, waits for them, and re-layouts  1.99 us (3%)
    pallas_call x1, Pallas kernels, body(): pl.pallas_call(kernel, out_shape=jax.ShapeDtypeStruct((q_rows, all_heads,...  72.9 us
    unnamed x1, local copies, waits for them, and re-layouts  1.99 us

profile of v2, /device:TPU:1, one launch (start us, length us, event | category | flops | bytes accessed | tf_op | source)
XLA Modules:
  0.0 74.9 jit_solution(16408768717843881085)
XLA Ops:
  0.0 72.9 %serve.1 = bf16[20,128,128]{2,1,0:T(8,128)(2,1)} custom-call(bf16[20,192,128]{2,1,0:T(8,128)(2,1)} %bitcast.5, bf16[160,576]{1,0:T(8,128)(2,1)} %latents_hbm.1, bf16[32,64,576]{2,1,0:T(8,128)(2,1)} %cache_hbm.1, bf16[16,128,512]{2,1,0:T(8,128)(2,1)} %key_up_hbm.1, bf16[16,512,128]{2,1,0:T(8,128)(2,1)} %value_up_hbm.1, s32[1,32]{1,0:T(1,128)} %bitcast.6, ...), custom_call_target="tpu_custom_call" | custom-call | tf_op jit(solution)/shard_map/serve/pallas_call | solution.py:475
  72.9 2.0 %copy.11 = bf16[20,128,128]{2,1,0:T(8,128)(2,1)} copy(bf16[20,128,128]{2,1,0:T(8,128)(2,1)} %serve.1) | data formatting | bytes 1310720

commit v3 on v2

--- a/solution.py
+++ b/solution.py
@@ -75,7 +75,7 @@
     out_ref,
     q_in, latents, cache, key_up, value_up, rows_here, table, ids,
     nope_out, rope_out, nope_in, rope_in, nope, rope, out0, out1, in0, in1, keys_a, keys_b,
-    query_p, query_d, mixed_p, mixed_d, values, values_out, seen, acc, peak, total,
+    query_p, query_d, mixed_p, mixed_d, values, values_out, seen, acc, peak, total, causal,
     local_sem, id_send, id_recv, nope_send, nope_recv, rope_send, rope_recv,
     send0, recv0, send1, recv1, a_send, a_recv, b_send, b_recv, out_send, out_recv, own_sem,
 ):
@@ -131,20 +131,6 @@
     lane = iota((nd, 128), 1)
     table[:, 0, :] = jnp.where(lane == 0, want0, jnp.where(lane == 1, want1, 0.0))
 
-    pl.semaphore_wait(barrier, nd - 1 + nh - 1)
-
-    def send_ids(step, carry):
-        peer = lax.rem(me + step, nd)
-        pltpu.make_async_remote_copy(
-            src_ref=table.at[peer], dst_ref=ids.at[me], send_sem=id_send, recv_sem=id_recv,
-            device_id=(peer, hd), device_id_type=MESH,
-        ).start()
-        return carry
-
-    lax.fori_loop(1, nd, send_ids, 0)
-    own_ids = pltpu.make_async_copy(table.at[me], ids.at[me], own_sem.at[0])
-    own_ids.start()
-
     loads[0].wait()
     half_heads = heads // 2
 
@@ -160,6 +146,26 @@
         return carry
 
     lax.fori_loop(0, q_rows // 2, turn, 0)
+
+    pre_row = iota((pre, 1), 0)
+    group = pre_row // q_rows
+    moved = jnp.where(group < front, 2 * group, 2 * (group - front) + 1) - group
+    pre_row = jnp.where(group < 2 * front, pre_row + moved * q_rows, pre_row)
+    causal[...] = jnp.where(iota((pre, pre), 1) <= pre_row, 0.0, HIDDEN)
+
+    pl.semaphore_wait(barrier, nd - 1 + nh - 1)
+
+    def send_ids(step, carry):
+        peer = lax.rem(me + step, nd)
+        pltpu.make_async_remote_copy(
+            src_ref=table.at[peer], dst_ref=ids.at[me], send_sem=id_send, recv_sem=id_recv,
+            device_id=(peer, hd), device_id_type=MESH,
+        ).start()
+        return carry
+
+    lax.fori_loop(1, nd, send_ids, 0)
+    own_ids = pltpu.make_async_copy(table.at[me], ids.at[me], own_sem.at[0])
+    own_ids.start()
 
     here = place_of(hd)
 
@@ -219,11 +225,13 @@
             row_copy(source, dest, send_sem, recv_sem, lax.rem(me + step, nd)).start()
             return carry
 
-        lax.fori_loop(1, nd, send_rows, 0)
+        if slot == 0: lax.fori_loop(1, nd, send_rows, 0)
         own = pltpu.make_async_copy(source.at[me], dest.at[me], own_sem.at[3 + slot])
         own.start()
         own_rows.append(own)
 
+    wait_bytes(in0.at[pl.ds(0, nd - 1)], send0)
+    lax.fori_loop(1, nd, send_rows, 0)
     for copy in own_q:
         copy.wait()
     loads[2].wait()
@@ -275,6 +283,29 @@
 
     gang_a = (keys_a, a_send, a_recv)
     gang_b = (keys_b, b_send, b_recv)
+
+    def give(device):
+        source = values_out.at[pl.ds(pl.multiple_of(place_of(jnp.int32(device)), 4), q_rows)]
+        dest = out_ref.at[:, pl.ds(pl.multiple_of(hd * heads, heads), heads), :]
+
+        @pl.when(hd != device)
+        def _():
+            pltpu.make_async_remote_copy(
+                src_ref=source, dst_ref=dest, send_sem=out_send, recv_sem=out_recv,
+                device_id=(me, device), device_id_type=MESH,
+            ).start()
+
+        @pl.when(hd == device)
+        def _():
+            pltpu.make_async_copy(source, dest, own_sem.at[5]).start()
+
+    def put_values(first, count, mixed, base):
+        for h in range(heads):
+            values[pl.ds(first * heads + h, count, stride=heads), :] = jnp.dot(
+                mixed[pl.ds(base + h * count, count), :], value_up[h], preferred_element_type=F32
+            )
+        done = values[pl.ds(first * heads, count * heads), :].astype(BF16)
+        values_out[pl.ds(first, count)] = done.reshape(count, heads, done.shape[1])
 
     own_rows[0].wait()
     wait_bytes(in0.at[pl.ds(0, nd - 1)], recv0)
@@ -291,7 +322,7 @@
     seen[...] = jnp.where((place >= 0.0) & (place < length), 0.0, HIDDEN)
     step_blocks = blocks // 4
     step_keys = step_blocks * block_rows
-    size_d = heads * dec // 2
+    size_d = heads * dec
 
     def decode_block(index, carry):
         at = pl.ds(pl.multiple_of(index * size_d, size_d), size_d)
@@ -315,37 +346,13 @@
         mixed_d[at, :] = (mixed / weight).astype(BF16)
         return carry
 
-    lax.fori_loop(0, 2, decode_block, 0)
-    share_on(*gang_a)
-
-    def give(device):
-        source = values_out.at[pl.ds(pl.multiple_of(place_of(jnp.int32(device)), 4), q_rows)]
-        dest = out_ref.at[:, pl.ds(pl.multiple_of(hd * heads, heads), heads), :]
-
-        @pl.when(hd != device)
-        def _():
-            pltpu.make_async_remote_copy(
-                src_ref=source, dst_ref=dest, send_sem=out_send, recv_sem=out_recv,
-                device_id=(me, device), device_id_type=MESH,
-            ).start()
-
-        @pl.when(hd == device)
-        def _():
-            pltpu.make_async_copy(source, dest, own_sem.at[5]).start()
-
-    def put_values(first, count, mixed, base):
-        for h in range(heads):
-            values[pl.ds(first * heads + h, count, stride=heads), :] = jnp.dot(
-                mixed[pl.ds(base + h * count, count), :], value_up[h], preferred_element_type=F32
-            )
-        done = values[pl.ds(first * heads, count * heads), :].astype(BF16)
-        values_out[pl.ds(first, count)] = done.reshape(count, heads, done.shape[1])
-
+    decode_block(0, 0)
     loads[5].wait()
     put_values(pre, dec, mixed_d, 0)
     give(nh - 1)
 
-    share_end(*gang_a)
+    share_on(*gang_a)
+
     own_rows[1].wait()
     wait_bytes(in1.at[pl.ds(0, nd - 1)], recv1)
     target = spread_rows(late, part)
@@ -355,28 +362,35 @@
     ).astype(BF16)
     share_own(*gang_b)
 
+    share_end(*gang_a)
+
     size = heads * part_rows // 2
-    key_count = reqs // 2 * block_rows
+
+    pieces = 2
+    piece = nh // pieces
+
+    def soften(kept, held, top):
+        weight, mixed = 0.0, 0.0
+        for x, keys in zip(kept, held):
+            raised = jnp.exp2(x * exponent - top)
+            weight += jnp.sum(raised, axis=1, keepdims=True)
+            mixed += jnp.dot(raised.astype(BF16), keys[:, :latent], preferred_element_type=F32)
+        return weight, mixed
+
+    def highest(kept):
+        return functools.reduce(jnp.maximum, [jnp.max(x, axis=1, keepdims=True) for x in kept]) * exponent
 
     def early_block(index, carry):
         at = pl.ds(pl.multiple_of(index * size, size), size)
         query = query_p[at, :]
-        local = latents[:pre, :]
-        keys = keys_a[...].reshape(key_count, width)
-        row = lax.rem(iota((size, pre), 0), part_rows) + (index // 2) * part_rows
-        group = row // q_rows
-        moved = jnp.where(group < front, 2 * group, 2 * (group - front) + 1) - group
-        row = jnp.where(group < 2 * front, row + moved * q_rows, row)
-        second = jnp.where(iota((size, pre), 1) <= row, scores(query, local), HIDDEN)
-        first = scores(query, keys)
-        top = jnp.maximum(
-            jnp.max(first, axis=1, keepdims=True), jnp.max(second, axis=1, keepdims=True)
-        ) * exponent
-        raised1 = jnp.exp2(first * exponent - top)
-        raised2 = jnp.exp2(second * exponent - top)
-        weight = jnp.sum(raised1, axis=1, keepdims=True) + jnp.sum(raised2, axis=1, keepdims=True)
-        mixed = jnp.dot(raised1.astype(BF16), keys[:, :latent], preferred_element_type=F32)
-        mixed += jnp.dot(raised2.astype(BF16), local[:, :latent], preferred_element_type=F32)
+        side = pl.ds(pl.multiple_of(index // 2 * part_rows, part_rows), part_rows)
+        held = [keys_a[j * piece:(j + 1) * piece].reshape(-1, width) for j in range(pieces)]
+        kept = [scores(query, keys) for keys in held]
+        held.append(latents[:pre, :])
+        own = scores(query, held[-1]).reshape(size // part_rows, part_rows, pre) + causal[side, :][None]
+        kept.append(own.reshape(size, pre))
+        top = highest(kept)
+        weight, mixed = soften(kept, held, top)
         acc[at, :] = mixed
         peak[at, :] = jnp.broadcast_to(top, (size, 128))
         total[at, :] = jnp.broadcast_to(weight, (size, 128))
@@ -384,27 +398,26 @@
 
     def late_block(index, carry):
         at = pl.ds(pl.multiple_of(index * size, size), size)
-        keys = keys_b[...].reshape(key_count, width)
-        first = scores(query_p[at, :], keys)
+        query = query_p[at, :]
+        held = [keys_b[j * piece:(j + 1) * piece].reshape(-1, width) for j in range(pieces)]
+        kept = [scores(query, keys) for keys in held]
         old = peak[at, :][:, 0:1]
-        top = jnp.maximum(old, jnp.max(first, axis=1, keepdims=True) * exponent)
+        top = jnp.maximum(old, highest(kept))
         fix = jnp.exp2(old - top)
-        raised = jnp.exp2(first * exponent - top)
-        weight = total[at, :][:, 0:1] * fix + jnp.sum(raised, axis=1, keepdims=True)
-        mixed = acc[at, :] * fix
-        mixed += jnp.dot(raised.astype(BF16), keys[:, :latent], preferred_element_type=F32)
-        mixed_p[at, :] = (mixed / weight).astype(BF16)
-        return carry
-
-    lax.fori_loop(0, 2, early_block, 0)
+        weight, mixed = soften(kept, held, top)
+        weight += total[at, :][:, 0:1] * fix
+        mixed_p[at, :] = ((acc[at, :] * fix + mixed) / weight).astype(BF16)
+        return carry
+
+    lax.fori_loop(0, 2, early_block, 0, unroll=True)
     share_on(*gang_b)
-    lax.fori_loop(2, 4, early_block, 0)
+    lax.fori_loop(2, 4, early_block, 0, unroll=True)
     share_end(*gang_b)
-    lax.fori_loop(0, 2, late_block, 0)
+    lax.fori_loop(0, 2, late_block, 0, unroll=True)
     put_values(0, part_rows, mixed_p, 0)
     for device in range(0, 2 * front, 2):
         give(device)
-    lax.fori_loop(2, 4, late_block, 0)
+    lax.fori_loop(2, 4, late_block, 0, unroll=True)
     put_values(part_rows, part_rows, mixed_p, heads * part_rows)
     for device in [*range(1, 2 * front, 2), *range(2 * front, nh - 1)]:
         give(device)
@@ -413,7 +426,6 @@
     share_sent(*gang_b)
     wait_bytes(nope_in.at[pl.ds(0, rows - q_rows)], nope_send)
     wait_bytes(rope_in.at[pl.ds(0, nh - 1)], rope_send)
-    wait_bytes(in0.at[pl.ds(0, nd - 1)], send0)
     wait_bytes(in1.at[pl.ds(0, nd - 1)], send1)
     wait_bytes(table.at[pl.ds(0, nd - 1)], id_send)
     wait_bytes(values_out.at[pl.ds(0, q_rows)], own_sem.at[5])
@@ -471,6 +483,7 @@
         ((pre * heads, latent), F32),
         ((pre * heads, 128), F32),
         ((pre * heads, 128), F32),
+        ((pre, pre), F32),
     ]
     return pl.pallas_call(
         kernel,

time: 75 us -> 68.3 us (0.911)
  Pallas kernels: 72.9 us -> 66.1 us
    pallas_call x1, Pallas kernels: 72.9 us -> 66.1 us  [body(): pl.pallas_call(kernel, out_shape=jax.ShapeDtypeStruct((q_rows, all_heads,...]
where the time goes in v3:
time: 68.3 us; the launch traced here: 68.1 us
  Pallas kernels  66.1 us (97%)
  local copies, waits for them, and re-layouts  1.99 us (3%)
    pallas_call x1, Pallas kernels, body(): pl.pallas_call(kernel, out_shape=jax.ShapeDtypeStruct((q_rows, all_heads,...  66.1 us
    unnamed x1, local copies, waits for them, and re-layouts  1.99 us

profile of v3, /device:TPU:1, one launch (start us, length us, event | category | flops | bytes accessed | tf_op | source)
XLA Modules:
  0.0 68.1 jit_solution(17421538234674001574)
XLA Ops:
  0.0 66.1 %serve.1 = bf16[20,128,128]{2,1,0:T(8,128)(2,1)} custom-call(bf16[20,192,128]{2,1,0:T(8,128)(2,1)} %bitcast.5, bf16[160,576]{1,0:T(8,128)(2,1)} %latents_hbm.1, bf16[32,64,576]{2,1,0:T(8,128)(2,1)} %cache_hbm.1, bf16[16,128,512]{2,1,0:T(8,128)(2,1)} %key_up_hbm.1, bf16[16,512,128]{2,1,0:T(8,128)(2,1)} %value_up_hbm.1, s32[1,32]{1,0:T(1,128)} %bitcast.6, ...), custom_call_target="tpu_custom_call" | custom-call | tf_op jit(solution)/shard_map/serve/pallas_call | solution.py:488
  66.1 2.0 %copy.11 = bf16[20,128,128]{2,1,0:T(8,128)(2,1)} copy(bf16[20,128,128]{2,1,0:T(8,128)(2,1)} %serve.1) | data formatting | bytes 1310720

commit v4 on v3

--- a/solution.py
+++ b/solution.py
@@ -256,30 +256,55 @@
         put_query(h, slice(latent, width), both[:, :rope_dim])
         put_query(h + half_heads, slice(latent, width), both[:, rope_dim:])
 
-    def share(keys, send_sem, recv_sem, index, peer, slot):
+    right, left = lax.rem(hd + 2, nh), lax.rem(hd - 2 + nh, nh)
+    far = lax.rem(hd + nh // 2, nh)
+    chunk_half = reqs * part // 4
+
+    def share(keys, send_sem, recv_sem, index, side, peer, slot):
+        span = keys.at[index, pl.ds(side * chunk_half, chunk_half)]
         return pltpu.make_async_remote_copy(
-            src_ref=keys.at[index], dst_ref=keys.at[index], send_sem=send_sem.at[slot],
-            recv_sem=recv_sem.at[index], device_id=(me, peer), device_id_type=MESH,
+            src_ref=span, dst_ref=span, send_sem=send_sem.at[slot],
+            recv_sem=recv_sem.at[index, side], device_id=(me, peer), device_id_type=MESH,
         )
 
     def share_own(*gang):
-        for step in range(1, chips):
-            share(*gang, hd, lax.rem(hd + 2 * step, nh), step).start()
-        share(*gang, hd, sibling, 0).start()
-
-    def share_on(*gang):
-        for step in range(1, chips):
-            source = lax.rem(hd - 2 * step + nh, nh)
-            share(*gang, source, sibling, 0).wait_recv()
-            share(*gang, source, sibling, chips + step).start()
-
-    def share_end(*gang):
-        for step in range(chips):
-            share(*gang, lax.rem(sibling + 2 * step, nh), sibling, 0).wait_recv()
+        for slot, (side, peer) in enumerate(
+            [(0, right), (1, left), (1, right), (0, left), (0, sibling), (1, sibling)]
+        ):
+            share(*gang, hd, side, peer, slot).start()
+
+    def landed(index, side, *gang):
+        share(*gang, index, side, sibling, 0).wait_recv()
+
+    def share_near(*gang):
+        landed(left, 0, *gang)
+        share(*gang, left, 0, right, 6).start()
+        share(*gang, left, 0, sibling, 7).start()
+        landed(right, 1, *gang)
+        share(*gang, right, 1, left, 8).start()
+        share(*gang, right, 1, sibling, 9).start()
+        landed(left, 1, *gang)
+        share(*gang, left, 1, sibling, 10).start()
+        landed(right, 0, *gang)
+        share(*gang, right, 0, sibling, 11).start()
+
+    def share_far(*gang):
+        for side in range(2):
+            landed(far, side, *gang)
+            share(*gang, far, side, sibling, 12 + side).start()
+
+    def near_here(*gang):
+        for step in (0, 2, nh - 2):
+            for side in range(2):
+                landed(lax.rem(sibling + step, nh), side, *gang)
+
+    def far_here(*gang):
+        for side in range(2):
+            landed(lax.rem(sibling + nh // 2, nh), side, *gang)
 
     def share_sent(*gang):
-        for slot in [*range(chips), *range(chips + 1, 2 * chips)]:
-            share(*gang, hd, sibling, slot).wait_send()
+        for slot in range(14):
+            share(*gang, hd, 0, sibling, slot).wait_send()
 
     gang_a = (keys_a, a_send, a_recv)
     gang_b = (keys_b, b_send, b_recv)
@@ -351,7 +376,7 @@
     put_values(pre, dec, mixed_d, 0)
     give(nh - 1)
 
-    share_on(*gang_a)
+    share_near(*gang_a)
 
     own_rows[1].wait()
     wait_bytes(in1.at[pl.ds(0, nd - 1)], recv1)
@@ -362,7 +387,9 @@
     ).astype(BF16)
     share_own(*gang_b)
 
-    share_end(*gang_a)
+    share_far(*gang_a)
+    near_here(*gang_a)
+    far_here(*gang_a)
 
     size = heads * part_rows // 2
 
@@ -410,9 +437,11 @@
         return carry
 
     lax.fori_loop(0, 2, early_block, 0, unroll=True)
-    share_on(*gang_b)
+    share_near(*gang_b)
     lax.fori_loop(2, 4, early_block, 0, unroll=True)
-    share_end(*gang_b)
+    share_far(*gang_b)
+    near_here(*gang_b)
+    far_here(*gang_b)
     lax.fori_loop(0, 2, late_block, 0, unroll=True)
     put_values(0, part_rows, mixed_p, 0)
     for device in range(0, 2 * front, 2):
@@ -491,7 +520,7 @@
         in_specs=[anywhere] * 5 + [vmem] * 4,
         out_specs=anywhere,
         scratch_shapes=[pltpu.VMEM(shape, dtype) for shape, dtype in buffers]
-        + [dma((6,))] + [dma] * 10 + [dma((nh,))] * 4 + [dma, dma, dma((6,))],
+        + [dma((6,))] + [dma] * 10 + [dma((14,)), dma((nh, 2))] * 2 + [dma, dma, dma((6,))],
         compiler_params=pltpu.CompilerParams(
             collective_id=0, has_side_effects=True, vmem_limit_bytes=60 * 2**20
         ),

time: 68.3 us -> 66.9 us (0.980)
  Pallas kernels: 66.1 us -> 64.8 us
    pallas_call x1, Pallas kernels: 66.1 us -> 64.8 us  [body(): pl.pallas_call(kernel, out_shape=jax.ShapeDtypeStruct((q_rows, all_heads,...]
where the time goes in v4:
time: 66.9 us; the launch traced here: 66.8 us
  Pallas kernels  64.8 us (97%)
  local copies, waits for them, and re-layouts  1.99 us (3%)
    pallas_call x1, Pallas kernels, body(): pl.pallas_call(kernel, out_shape=jax.ShapeDtypeStruct((q_rows, all_heads,...  64.8 us
    unnamed x1, local copies, waits for them, and re-layouts  1.99 us

profile of v4, /device:TPU:1, one launch (start us, length us, event | category | flops | bytes accessed | tf_op | source)
XLA Modules:
  0.0 66.8 jit_solution(5055153915005298377)
XLA Ops:
  0.0 64.8 %serve.1 = bf16[20,128,128]{2,1,0:T(8,128)(2,1)} custom-call(bf16[20,192,128]{2,1,0:T(8,128)(2,1)} %bitcast.5, bf16[160,576]{1,0:T(8,128)(2,1)} %latents_hbm.1, bf16[32,64,576]{2,1,0:T(8,128)(2,1)} %cache_hbm.1, bf16[16,128,512]{2,1,0:T(8,128)(2,1)} %key_up_hbm.1, bf16[16,512,128]{2,1,0:T(8,128)(2,1)} %value_up_hbm.1, s32[1,32]{1,0:T(1,128)} %bitcast.6, ...), custom_call_target="tpu_custom_call" | custom-call | tf_op jit(solution)/shard_map/serve/pallas_call | solution.py:517
  64.8 2.0 %copy.11 = bf16[20,128,128]{2,1,0:T(8,128)(2,1)} copy(bf16[20,128,128]{2,1,0:T(8,128)(2,1)} %serve.1) | data formatting | bytes 1310720
